TPU v7x, 32 devices: a whole 2x2x4 slice. The times are simulated.
32 devices in a mesh: dp: 16 (over z, y, x), ctx: 2 (over core).
Axes of the slice: x: 2, y: 2, z: 4, core: 2. Of those that a mesh axis runs over, the one named last changes fastest.
Arguments:
- queries: bfloat16 [4096, 4096], P(('dp', 'ctx')), may hold values from -150 to 150
- keys: bfloat16 [4096, 512], P(('dp', 'ctx')), may hold values from -4 to 4
- values: bfloat16 [4096, 512], P(('dp', 'ctx')), may hold values from -6 to 6
- lengths: int32 [32], replicated, may hold values from 1 to 512, 4096 in all
Outputs:
- attended: bfloat16 [4096, 4096], P(('dp', 'ctx'))
Inputs may be any that keep to these rules, and one draw needn't show every extreme that they name: lengths of the 32 documents sum to 4096; the largest is exactly 512.
All inputs are finite; a program needn't handle non-finite values.
Results may differ from a plain program's by a relative error of at most 0.0045.
Values may be sent and summed in bfloat16 or wider, within the bound.
No kernel may reach another device: no remote copies, remote signals or barrier semaphores. Data moves between devices by JAX's collectives and lax.ppermute only.
A program may use at most 128 MiB of HBM per device.

v0:
```python
import functools
import math

import jax
import jax.numpy as jnp
from jax import lax
from jax.experimental import pallas as pl
from jax.experimental.pallas import tpu as pltpu
from jax.sharding import PartitionSpec as P

HEAD_SIZE = 128
QUERY_HEADS = 32
KEY_VALUE_HEADS = 4
GROUP = QUERY_HEADS // KEY_VALUE_HEADS
HEADS_AT_ONCE = 4
EARLY_CHAINS = 4
EXCLUDED = -1e30
PAD = 16
AXES = ("dp", "ctx")


FACTOR = math.log2(math.e) / math.sqrt(HEAD_SIZE)


def head_columns(i):
    return slice(i * HEAD_SIZE, (i + 1) * HEAD_SIZE)


def stacked(ref, heads, rows):
    return jnp.concatenate([ref[:rows, head_columns(i)] for i in heads], axis=0)


def spread(ref, heads, rows, value):
    for n, i in enumerate(heads):
        ref[:rows, head_columns(i)] = value[n * rows : (n + 1) * rows].astype(ref.dtype)


def with_ones(value):
    return jnp.concatenate([value, jnp.ones(value.shape, value.dtype)], axis=1)


def scores_of(q, key, bias):
    scores = lax.dot_general(
        q, key, (((1,), (1,)), ((), ())), preferred_element_type=jnp.float32
    )
    return scores + jnp.concatenate([bias] * (q.shape[0] // bias.shape[0]), axis=0)


def weights_of(scores, top):
    return jnp.exp2((scores - top) * jnp.float32(FACTOR)).astype(jnp.bfloat16)


def normalised(summed, total):
    inverse = pl.reciprocal(total, approx=True)
    return summed * (inverse * (2.0 - total * inverse))


def level_of(top, total):
    return top + jnp.log(total) * jnp.float32(math.sqrt(HEAD_SIZE))


def chains(size=HEADS_AT_ONCE):
    return [(range(h, h + size), h // GROUP) for h in range(0, QUERY_HEADS, size)]


def in_turn(runs, *stages):
    results = {}
    for turn in range(len(runs) + len(stages) - 1):
        for n, stage in enumerate(stages):
            i = turn - n
            if 0 <= i < len(runs):
                results[i] = stage(*runs[i], *results.pop(i, ()))


def pack_kernel(key_hbm, value_hbm, out_ref, sems):
    rows = key_hbm.shape[0]
    copies = [
        pltpu.make_async_copy(key_hbm, out_ref.at[:rows], sems.at[0]),
        pltpu.make_async_copy(value_hbm, out_ref.at[rows:], sems.at[1]),
    ]
    for copy in copies:
        copy.start()
    for copy in copies:
        copy.wait()


def pack(keys, values):
    rows, width = keys.shape
    return pl.pallas_call(
        pack_kernel,
        out_shape=pltpu.VMEM((2 * rows, width), keys.dtype),
        in_specs=[HBM, HBM],
        out_specs=VMEM,
        scratch_shapes=[pltpu.SemaphoreType.DMA((2,))],
        compiler_params=pltpu.CompilerParams(vmem_limit_bytes=1024 * 1024),
    )(*in_hbm(keys, values))


def attend_own(runs, rows, own_ref, own_bias_ref, q_ref, level_ref, mean_ref, ready):
    def match(heads, g):
        ready(heads, g)
        key = own_ref[:rows, head_columns(g)]
        return (scores_of(stacked(q_ref, heads, rows), key, own_bias_ref[...]),)

    def weigh(heads, g, scores):
        top = jnp.max(scores, axis=1, keepdims=True)
        return weights_of(scores, top), jnp.broadcast_to(top, scores.shape)

    def gather(heads, g, weights, top):
        value = with_ones(own_ref[rows:, head_columns(g)])
        more = jnp.dot(weights, value, preferred_element_type=jnp.float32)
        summed, total = more[:, :HEAD_SIZE], more[:, HEAD_SIZE:]
        spread(mean_ref, heads, rows, normalised(summed, total))
        spread(level_ref, heads, rows, level_of(top, total))

    in_turn(runs, match, weigh, gather)


def own_kernel(
    rounds, rows, own_ref, lengths_hbm, q_hbm,
    longer_ref, bias_ref, needed_ref, own_bias_ref, q_ref, odd_ref, level_ref, mean_ref,
    lengths_ref, lengths_sem, q_sems,
):
    lengths_copy = pltpu.make_async_copy(lengths_hbm, lengths_ref, lengths_sem)
    lengths_copy.start()
    width = GROUP * HEAD_SIZE
    q_copies = []
    for g in range(KEY_VALUE_HEADS):
        at = slice(g * width, (g + 1) * width)
        q_copies.append(pltpu.make_async_copy(q_hbm.at[:, at], q_ref.at[:, at], q_sems.at[g]))
        q_copies[g].start()
    me = lax.axis_index("dp") * lax.axis_size("ctx") + lax.axis_index("ctx")
    longer_ref[: 2 * rows, :] = own_ref[...]
    longer_ref[2 * rows :, :] = jnp.zeros((PAD, longer_ref.shape[1]), longer_ref.dtype)
    odd_ref[...] = jnp.full(odd_ref.shape, lax.rem(me, 2), jnp.int32)
    first = me * rows
    query_pos = first + lax.broadcasted_iota(jnp.int32, (rows, rows), 0)
    lengths_copy.wait()

    def later(doc, carried):
        bound, start, first_start, first_end = carried
        following = bound + lengths_ref[doc]
        start = jnp.where(query_pos >= bound, bound, start)
        first_start = jnp.where(first >= bound, bound, first_start)
        first_end = jnp.where(first >= bound, following, first_end)
        return following, start, first_start, first_end

    zero = jnp.int32(0)
    _, start, first_start, first_end = lax.fori_loop(
        0,
        lengths_ref.shape[0],
        later,
        (zero, jnp.zeros((rows, rows), jnp.int32), zero, zero),
        unroll=8,
    )
    needed = lax.div(first - first_start + (rows - 1), jnp.int32(rows))
    crossing = jnp.minimum(first_end - first, rows)
    needed_ref[...] = jnp.full(needed_ref.shape, needed * (rows + 1) + crossing, jnp.int32)
    lane = lax.broadcasted_iota(jnp.int32, (rows, rows), 1)

    def bias_of(allowed):
        return jnp.where(allowed, jnp.float32(0.0), jnp.float32(EXCLUDED))

    key_pos = first + lane
    own_bias_ref[...] = bias_of((key_pos >= start) & (key_pos <= query_pos))
    for b in range(2 * rounds):
        key_pos = first - (b + 1) * rows + lane
        bias_ref[:, b * rows : (b + 1) * rows] = bias_of(key_pos >= start)

    def ready(heads, g):
        if heads[0] % GROUP == 0:
            q_copies[g].wait()

    runs = chains()[:EARLY_CHAINS]
    attend_own(runs, rows, own_ref, own_bias_ref, q_ref, level_ref, mean_ref, ready)
    for copy in q_copies[runs[-1][1] + 1 :]:
        copy.wait()


def own_rest_kernel(
    rows, own_ref, own_bias_ref, q_ref, odd_ref, *parts
):
    runs = chains()[EARLY_CHAINS:]
    parts = parts[3:]
    attend_own(runs, rows, own_ref, own_bias_ref, q_ref, *parts, lambda heads, g: None)


def in_vmem(*operands):
    return [pltpu.with_memory_space_constraint(x, pltpu.VMEM) for x in operands]


def in_hbm(*operands):
    return [pltpu.with_memory_space_constraint(x, pltpu.HBM) for x in operands]


SMEM = pl.BlockSpec(memory_space=pltpu.SMEM)
VMEM = pl.BlockSpec(memory_space=pltpu.VMEM)
HBM = pl.BlockSpec(memory_space=pltpu.HBM)


def own_part(lengths, queries, own, rounds):
    rows = queries.shape[0]
    part = pltpu.VMEM(queries.shape, jnp.float32)
    return pl.pallas_call(
        functools.partial(own_kernel, rounds, rows),
        out_shape=(
            pltpu.VMEM((2 * rows + PAD, own.shape[1]), own.dtype),
            pltpu.VMEM((rows, 2 * rounds * rows), jnp.float32),
            pltpu.VMEM((8, 128), jnp.int32),
            pltpu.VMEM((rows, rows), jnp.float32),
            pltpu.VMEM(queries.shape, queries.dtype),
            pltpu.VMEM((1, own.shape[1]), jnp.int32),
            part,
            part,
        ),
        in_specs=[VMEM, HBM, HBM],
        out_specs=(VMEM,) * 8,
        scratch_shapes=[
            pltpu.SMEM(lengths.shape, jnp.int32),
            pltpu.SemaphoreType.DMA,
            pltpu.SemaphoreType.DMA((KEY_VALUE_HEADS,)),
        ],
        compiler_params=pltpu.CompilerParams(vmem_limit_bytes=10 * 1024 * 1024),
        cost_estimate=pl.CostEstimate(
            flops=4 * 10**9, bytes_accessed=16 * 10**6, transcendentals=rows * queries.size
        ),
    )(*in_vmem(own), *in_hbm(lengths, queries))


def own_rest(own, own_bias, queries, kept):
    rows = queries.shape[0]
    operands = in_vmem(own, own_bias, queries, *kept)
    return pl.pallas_call(
        functools.partial(own_rest_kernel, rows),
        out_shape=tuple(pltpu.VMEM(x.shape, x.dtype) for x in kept),
        in_specs=[VMEM] * len(operands),
        out_specs=(VMEM,) * len(kept),
        input_output_aliases={3 + n: n for n in range(len(kept))},
        compiler_params=pltpu.CompilerParams(vmem_limit_bytes=10 * 1024 * 1024),
        cost_estimate=pl.CostEstimate(
            flops=4 * 10**9, bytes_accessed=16 * 10**6, transcendentals=rows * queries.size
        ),
    )(*operands)


def behind_kernel(
    before, last, rows, needed_ref, bias_ref, q_ref, near_ref, further_ref, level_ref, mean_ref, *refs
):
    both = needed_ref[0, 0]
    beyond = lax.div(both, rows + 1) - before
    crossing = lax.rem(both, rows + 1)
    pairs = [(ref.at[:rows], ref.at[rows : 2 * rows]) for ref in (near_ref, further_ref)]
    if last:
        out_hbm, out_ref, out_sems = refs

        def out_copy(n):
            width = HEADS_AT_ONCE * HEAD_SIZE
            at = slice(n * width, (n + 1) * width)
            return pltpu.make_async_copy(out_ref.at[:, at], out_hbm.at[:, at], out_sems.at[n])

    else:
        _, new_level_ref, new_mean_ref = refs

    def finish(heads, upto, mean):
        spread(out_ref, heads, upto, mean)
        if upto < rows:
            for i in heads:
                out_ref[upto:, head_columns(i)] = mean_ref[upto:, head_columns(i)].astype(
                    out_ref.dtype
                )
        for i in heads[::HEADS_AT_ONCE]:
            out_copy(i // HEADS_AT_ONCE).start()

    def attend(count, upto):
        def match(heads, g):
            key = jnp.concatenate([key[:, head_columns(g)] for key, _ in pairs[:count]], axis=0)
            bias = bias_ref[:upto, before * rows : (before + count) * rows]
            return (scores_of(stacked(q_ref, heads, upto), key, bias),)

        def weigh(heads, g, scores):
            level = stacked(level_ref, heads, upto)
            top = jnp.maximum(level, jnp.max(scores, axis=1, keepdims=True))
            fade = jnp.exp2((level - top) * jnp.float32(FACTOR))
            return weights_of(scores, jnp.concatenate([top] * count, axis=1)), fade, top

        def gather(heads, g, weights, fade, top):
            value = jnp.concatenate([value[:, head_columns(g)] for _, value in pairs[:count]], axis=0)
            more = jnp.dot(weights, with_ones(value), preferred_element_type=jnp.float32)
            summed = stacked(mean_ref, heads, upto) * fade + more[:, :HEAD_SIZE]
            total = fade + more[:, HEAD_SIZE:]
            if last:
                finish(heads, upto, normalised(summed, total))
            else:
                spread(new_mean_ref, heads, upto, normalised(summed, total))
                spread(new_level_ref, heads, upto, level_of(top, total))

        runs = chains() if upto == rows else chains(GROUP)
        in_turn(runs, match, weigh, gather)

    short = crossing <= rows // 2
    pl.when((beyond > 0) & short)(functools.partial(attend, 2, rows // 2))
    pl.when((beyond > 1) & jnp.logical_not(short))(functools.partial(attend, 2, rows))
    pl.when((beyond == 1) & jnp.logical_not(short))(functools.partial(attend, 1, rows))

    if last:
        @pl.when(beyond < 1)
        def _():
            in_turn(
                chains(),
                lambda heads, g: finish(heads, rows, stacked(mean_ref, heads, rows)),
            )

        for n in range(len(chains())):
            out_copy(n).wait()


def behind_part(before, last, needed, bias, queries, near, further, parts):
    rows = queries.shape[0]
    area = rows * rows * 2 * QUERY_HEADS
    operands = in_vmem(needed, bias, queries, near, further, *parts)
    if last:
        out_shape = jax.ShapeDtypeStruct(queries.shape, queries.dtype)
        out_specs = HBM
        scratch = [
            pltpu.VMEM(queries.shape, queries.dtype),
            pltpu.SemaphoreType.DMA((len(chains()),)),
        ]
        aliases = {}
    else:
        kept = (further, *parts)
        out_shape = tuple(pltpu.VMEM(part.shape, part.dtype) for part in kept)
        out_specs = (VMEM,) * len(kept)
        scratch = []
        aliases = {4 + n: n for n in range(len(kept))}
    return pl.pallas_call(
        functools.partial(behind_kernel, before, last, rows),
        out_shape=out_shape,
        in_specs=[VMEM] * len(operands),
        out_specs=out_specs,
        scratch_shapes=scratch,
        input_output_aliases=aliases,
        compiler_params=pltpu.CompilerParams(vmem_limit_bytes=10 * 1024 * 1024),
        cost_estimate=pl.CostEstimate(
            flops=4 * area, bytes_accessed=queries.size, transcendentals=0
        ),
    )(*operands)


def per_device(queries, keys, values, lengths):
    count = lax.axis_size("dp") * lax.axis_size("ctx")
    rounds = lax.axis_size("ctx")

    def from_behind(block, r):
        by = 2 * (r + 1)
        return lax.ppermute(block, AXES, [(i, i + by) for i in range(count - by)])

    own = pack(keys, values)
    fetched = [from_behind(own, 0)]
    longer, bias, needed, own_bias, queries, *kept = own_part(lengths, queries, own, rounds)
    fetched += [from_behind(longer, r) for r in range(1, rounds)]
    odd, *parts = own_rest(own, own_bias, queries, kept)
    swap = [(i, i ^ 1) for i in range(count)]
    nearer = own
    size = 2 * keys.shape[0]
    for r, further in enumerate(fetched):
        last = r == rounds - 1
        near = lax.ppermute(jnp.where(odd == 1, further[:size], nearer[:size]), AXES, swap)
        result = behind_part(2 * r, last, needed, bias, queries, near, further, parts)
        if not last:
            nearer, *parts = result
    return result


def solution(mesh):
    in_specs = (P(AXES, None), P(AXES, None), P(AXES, None), P())
    return jax.shard_map(
        per_device, mesh=mesh, in_specs=in_specs, out_specs=P(AXES, None), check_vma=False
    )
```

profile of v0, /device:TPU:8, one launch (start us, length us, event | category | flops | bytes accessed | tf_op | source)
XLA Modules:
  0.0 23.1 jit_solution(1888059294913756381)
XLA Ops:
  0.0 1.0 %shard_map.46.own_ref = bf16[256,512]{1,0:T(8,128)(2,1)S(1)} custom-call(bf16[128,512]{1,0:T(8,128)(2,1)} %key_hbm.1, bf16[128,512]{1,0:T(8,128)(2,1)} %value_hbm.1), custom_call_target="tpu_custom_call" | custom-call | tf_op jit(solution)/shard_map/pallas_call | solution.py:89
  1.0 3.4 %collective-permute-start.1 = (bf16[256,512]{1,0:T(8,128)(2,1)S(1)}, bf16[256,512]{1,0:T(8,128)(2,1)S(1)}, u32[]{:S(2)}, u32[]{:S(2)}) collective-permute-start(bf16[256,512]{1,0:T(8,128)(2,1)S(1)} %shard_map.46.own_ref), channel_id=1, source_target_pairs={{0,2},{1,3},{2,4},{3,5},{4,6},{5,7},{6,8},{7,9},{8,10},{9,11},{10,... | collective-permute-start | bytes 786440 | tf_op jit(solution)/shard_map/ppermute | solution.py:355
  4.4 2.1 %shard_map.47 = (bf16[272,512]{1,0:T(8,128)(2,1)S(1)}, f32[128,512]{1,0:T(8,128)S(1)}, s32[8,128]{1,0:T(8,128)S(1)}, f32[128,128]{1,0:T(8,128)S(1)}, bf16[128,40...) custom-call(bf16[256,512]{1,0:T(8,128)(2,1)S(1)} %shard_map.46.own_ref, ...), custom_call_target="tpu_custom_call" | custom-call | flops 4000000000 | bytes 16000000 | tf_op jit(solution)/shard_map/pallas_call | solution.py:204
  6.5 3.4 %collective-permute-start = (bf16[272,512]{1,0:T(8,128)(2,1)S(1)}, bf16[272,512]{1,0:T(8,128)(2,1)S(1)}, u32[]{:S(2)}, u32[]{:S(2)}) collective-permute-start(bf16[272,512]{1,0:T(8,128)(2,1)S(1)} %get-tuple-element.27), channel_id=1, source_target_pairs={{0,4},{1,5},{2,6},{3,7},{4,8},{5,9},{6,10},{7,11},{8,12},{9,13},{1... | collective-permute-start | bytes 835592 | tf_op jit(solution)/shard_map/ppermute | solution.py:355
  9.9 0.9 %shard_map.48 = (s32[1,512]{1,0:T(1,128)S(1)}, f32[128,4096]{1,0:T(8,128)S(1)}, f32[128,4096]{1,0:T(8,128)S(1)}) custom-call(bf16[256,512]{1,0:T(8,128)(2,1)S(1)} %shard_map.46.own_ref, f32[128,128]{1,0:T(8,128)S(1)} %get-tuple-element.22.own_bias_ref, ...), custom_call_target="tpu_custom_call", output_to_operand_aliasing={{0}: (3, {}), {1}: (4, {}), {2}: (5, {})} | custom-call | flops 4000000000 | bytes 16000000 | tf_op jit(solution)/shard_map/pallas_call | solution.py:233
  10.8 3.3 %collective-permute-done.1.further_ref = bf16[256,512]{1,0:T(8,128)(2,1)S(1)} collective-permute-done((bf16[256,512]{1,0:T(8,128)(2,1)S(1)}, bf16[256,512]{1,0:T(8,128)(2,1)S(1)}, u32[]{:S(2)}, u32[]{:S(2)}) %collective-permute-start.1) | collective-permute-done | bytes 262176 | tf_op jit(solution)/shard_map/ppermute | solution.py:355
  14.1 0.1 collective-permute-start.2
  14.2 1.5 %collective-permute-done.2.near_ref = bf16[256,512]{1,0:T(8,128)(2,1)S(1)} collective-permute-done((bf16[256,512]{1,0:T(8,128)(2,1)S(1)}, bf16[256,512]{1,0:T(8,128)(2,1)S(1)}, u32[]{:S(2)}, u32[]{:S(2)}) %collective-permute-start.2) | collective-permute-done | bytes 262176 | tf_op jit(solution)/shard_map/ppermute | solution.py:367
  15.7 2.9 %shard_map.49 = (bf16[256,512]{1,0:T(8,128)(2,1)S(1)}, f32[128,4096]{1,0:T(8,128)S(1)}, f32[128,4096]{1,0:T(8,128)S(1)}) custom-call(s32[8,128]{1,0:T(8,128)S(1)} %get-tuple-element.19.needed_ref, f32[128,512]{1,0:T(8,128)S(1)} %get-tuple-element.20.bias_ref, ...), custom_call_target="tpu_custom_call", output_to_operand_aliasing={{0}: (4, {}), {1}: (5, {}), {2}: (6, {})} | custom-call | flops 4194304 | bytes 524288 | tf_op jit(solution)/shard_map/pallas_call | solution.py:335
  18.6 0.1 collective-permute-done.further_ref
  18.7 0.1 collective-permute-start.3
  18.8 1.5 %collective-permute-done.3.near_ref = bf16[256,512]{1,0:T(8,128)(2,1)S(1)} collective-permute-done((bf16[256,512]{1,0:T(8,128)(2,1)S(1)}, bf16[256,512]{1,0:T(8,128)(2,1)S(1)}, u32[]{:S(2)}, u32[]{:S(2)}) %collective-permute-start.3) | collective-permute-done | bytes 262176 | tf_op jit(solution)/shard_map/ppermute | solution.py:367
  20.3 2.8 %shard_map.50 = bf16[128,4096]{1,0:T(8,128)(2,1)} custom-call(s32[8,128]{1,0:T(8,128)S(1)} %get-tuple-element.19.needed_ref, f32[128,512]{1,0:T(8,128)S(1)} %get-tuple-element.20.bias_ref, bf16[128,4096]{1,0:T(8,128)(2,1)S(1)} %get-tuple-element.21.q_ref, bf16[256,512]{1,0:T(8,128)(2,1)S(1)} %collective-permute-done.3.near_ref, ...), custom_call_target="tpu_custom_call" | custom-call | flops 4194304 | bytes 524288 | tf_op jit(solution)/shard_map/pallas_call | solution.py:335
  (3 shorter events, 0.1 us)
Async XLA Ops:
  1.0 13.1 %collective-permute-start.1 = (bf16[256,512]{1,0:T(8,128)(2,1)S(1)}, bf16[256,512]{1,0:T(8,128)(2,1)S(1)}, u32[]{:S(2)}, u32[]{:S(2)}) collective-permute-start(bf16[256,512]{1,0:T(8,128)(2,1)S(1)} %shard_map.46.own_ref), channel_id=1, source_target_pairs={{0,2},{1,3},{2,4},{3,5},{4,6},{5,7},{6,8},{7,9},{8,10},{9,11},{10,... | collective-permute-start | bytes 786440 | tf_op jit(solution)/shard_map/ppermute | solution.py:355
  6.5 12.2 %collective-permute-start = (bf16[272,512]{1,0:T(8,128)(2,1)S(1)}, bf16[272,512]{1,0:T(8,128)(2,1)S(1)}, u32[]{:S(2)}, u32[]{:S(2)}) collective-permute-start(bf16[272,512]{1,0:T(8,128)(2,1)S(1)} %get-tuple-element.27), channel_id=1, source_target_pairs={{0,4},{1,5},{2,6},{3,7},{4,8},{5,9},{6,10},{7,11},{8,12},{9,13},{1... | collective-permute-start | bytes 835592 | tf_op jit(solution)/shard_map/ppermute | solution.py:355
  14.1 1.6 %collective-permute-start.2 = (bf16[256,512]{1,0:T(8,128)(2,1)S(1)}, bf16[256,512]{1,0:T(8,128)(2,1)S(1)}, u32[]{:S(2)}, u32[]{:S(2)}) collective-permute-start(bf16[256,512]{1,0:T(8,128)(2,1)S(1)} %broadcast_select_fusion), channel_id=1, source_target_pairs={{0,1},{1,0},{2,3},{3,2},{4,5},{5,4},{6,7},{7,6},{8,9},{9,8},{10,11... | collective-permute-start | bytes 786440 | tf_op jit(solution)/shard_map/ppermute | solution.py:367
  18.7 1.6 %collective-permute-start.3 = (bf16[256,512]{1,0:T(8,128)(2,1)S(1)}, bf16[256,512]{1,0:T(8,128)(2,1)S(1)}, u32[]{:S(2)}, u32[]{:S(2)}) collective-permute-start(bf16[256,512]{1,0:T(8,128)(2,1)S(1)} %slice_select_fusion), channel_id=1, source_target_pairs={{0,1},{1,0},{2,3},{3,2},{4,5},{5,4},{6,7},{7,6},{8,9},{9,8},{10,11... | collective-permute-start | bytes 786440 | tf_op jit(solution)/shard_map/ppermute | solution.py:367
where the time goes:
time: 23.3 us; the launch traced here: 23.1 us
  Pallas kernels  9.59 us (41%)
  starting transfers between devices  6.97 us (30%)
  waiting for transfers between devices  6.37 us (27%)
    ppermute x2, starting transfers between devices, from_behind(): return lax.ppermute(block, AXES, [(i, i + by) for i in range(count - by)])  6.83 us
    pallas_call x2, Pallas kernels, behind_part(): pl.pallas_call(functools.partial(behind_kernel, before, last, rows), out_...  5.68 us
    ppermute x2, waiting for transfers between devices, from_behind(): return lax.ppermute(block, AXES, [(i, i + by) for i in range(count - by)])  3.33 us
    ppermute x2, waiting for transfers between devices, per_device(): lax.ppermute(jnp.where(odd == 1, further[:size], nearer[:size]), AXES, swap)  3.04 us
    pallas_call x1, Pallas kernels, own_part(): pl.pallas_call(functools.partial(own_kernel, rounds, rows), out_shape=(pl...  2.05 us
    pallas_call x1, Pallas kernels, pack(): pl.pallas_call(pack_kernel, out_shape=pltpu.VMEM((2 * rows, width), keys....  0.98 us
    pallas_call x1, Pallas kernels, own_rest(): pl.pallas_call(functools.partial(own_rest_kernel, rows), out_shape=tuple(...  0.88 us
  transfers between devices with their start and end apart: 4, of which 4 were waited for; matrix products, arithmetic and copies ran while one was open for 0% of the time, Pallas kernels for 25%

commit v1 on v0

--- a/solution.py
+++ b/solution.py
@@ -35,10 +35,6 @@
         ref[:rows, head_columns(i)] = value[n * rows : (n + 1) * rows].astype(ref.dtype)
 
 
-def with_ones(value):
-    return jnp.concatenate([value, jnp.ones(value.shape, value.dtype)], axis=1)
-
-
 def scores_of(q, key, bias):
     scores = lax.dot_general(
         q, key, (((1,), (1,)), ((), ())), preferred_element_type=jnp.float32
@@ -47,7 +43,9 @@
 
 
 def weights_of(scores, top):
-    return jnp.exp2((scores - top) * jnp.float32(FACTOR)).astype(jnp.bfloat16)
+    weights = jnp.exp2((scores - top) * jnp.float32(FACTOR))
+    total = jnp.sum(weights, axis=1, keepdims=True)
+    return weights.astype(jnp.bfloat16), jnp.broadcast_to(total, (scores.shape[0], HEAD_SIZE))
 
 
 def normalised(summed, total):
@@ -104,12 +102,11 @@
 
     def weigh(heads, g, scores):
         top = jnp.max(scores, axis=1, keepdims=True)
-        return weights_of(scores, top), jnp.broadcast_to(top, scores.shape)
-
-    def gather(heads, g, weights, top):
-        value = with_ones(own_ref[rows:, head_columns(g)])
-        more = jnp.dot(weights, value, preferred_element_type=jnp.float32)
-        summed, total = more[:, :HEAD_SIZE], more[:, HEAD_SIZE:]
+        return *weights_of(scores, top), jnp.broadcast_to(top, scores.shape)
+
+    def gather(heads, g, weights, total, top):
+        value = own_ref[rows:, head_columns(g)]
+        summed = jnp.dot(weights, value, preferred_element_type=jnp.float32)
         spread(mean_ref, heads, rows, normalised(summed, total))
         spread(level_ref, heads, rows, level_of(top, total))
 
@@ -281,13 +278,13 @@
             level = stacked(level_ref, heads, upto)
             top = jnp.maximum(level, jnp.max(scores, axis=1, keepdims=True))
             fade = jnp.exp2((level - top) * jnp.float32(FACTOR))
-            return weights_of(scores, jnp.concatenate([top] * count, axis=1)), fade, top
-
-        def gather(heads, g, weights, fade, top):
+            return *weights_of(scores, jnp.concatenate([top] * count, axis=1)), fade, top
+
+        def gather(heads, g, weights, total, fade, top):
             value = jnp.concatenate([value[:, head_columns(g)] for _, value in pairs[:count]], axis=0)
-            more = jnp.dot(weights, with_ones(value), preferred_element_type=jnp.float32)
-            summed = stacked(mean_ref, heads, upto) * fade + more[:, :HEAD_SIZE]
-            total = fade + more[:, HEAD_SIZE:]
+            more = jnp.dot(weights, value, preferred_element_type=jnp.float32)
+            summed = stacked(mean_ref, heads, upto) * fade + more
+            total = fade + total
             if last:
                 finish(heads, upto, normalised(summed, total))
             else:

time: 23.3 us -> 23.8 us (1.021)
  the two profiles are of different devices: /device:TPU:8 before, /device:TPU:25 now
where the time goes in v1:
time: 23.8 us
  Pallas kernels  9.87 us (41%)
  starting transfers between devices  9.66 us (41%)
  waiting for transfers between devices  3.93 us (17%)
    ppermute x2, starting transfers between devices, from_behind(): return lax.ppermute(block, AXES, [(i, i + by) for i in range(count - by)])  6.27 us
    pallas_call x2, Pallas kernels, behind_part(): pl.pallas_call(functools.partial(behind_kernel, before, last, rows), out_...  5.95 us
    ppermute x2, starting transfers between devices, per_device(): lax.ppermute(jnp.where(odd == 1, further[:size], nearer[:size]), AXES, swap)  3.39 us
    ppermute x2, waiting for transfers between devices, per_device(): lax.ppermute(jnp.where(odd == 1, further[:size], nearer[:size]), AXES, swap)  2.32 us
    pallas_call x1, Pallas kernels, own_part(): pl.pallas_call(functools.partial(own_kernel, rounds, rows), out_shape=(pl...  2.05 us
    ppermute x2, waiting for transfers between devices, from_behind(): return lax.ppermute(block, AXES, [(i, i + by) for i in range(count - by)])  1.61 us
    pallas_call x1, Pallas kernels, pack(): pl.pallas_call(pack_kernel, out_shape=pltpu.VMEM((2 * rows, width), keys....  0.98 us
    pallas_call x1, Pallas kernels, own_rest(): pl.pallas_call(functools.partial(own_rest_kernel, rows), out_shape=tuple(...  0.89 us
  transfers between devices with their start and end apart: 4, of which 3 were waited for; matrix products, arithmetic and copies ran while one was open for 0% of the time, Pallas kernels for 25%

profile of v1, /device:TPU:25, one launch (start us, length us, event | category | flops | bytes accessed | tf_op | source)
XLA Modules:
  0.0 23.8 jit_solution(14569239954432126228)
XLA Ops:
  0.0 1.0 %shard_map.46.own_ref = bf16[256,512]{1,0:T(8,128)(2,1)S(1)} custom-call(bf16[128,512]{1,0:T(8,128)(2,1)} %key_hbm.1, bf16[128,512]{1,0:T(8,128)(2,1)} %value_hbm.1), custom_call_target="tpu_custom_call" | custom-call | tf_op jit(solution)/shard_map/pallas_call | solution.py:87
  1.0 3.1 %collective-permute-start.1 = (bf16[256,512]{1,0:T(8,128)(2,1)S(1)}, bf16[256,512]{1,0:T(8,128)(2,1)S(1)}, u32[]{:S(2)}, u32[]{:S(2)}) collective-permute-start(bf16[256,512]{1,0:T(8,128)(2,1)S(1)} %shard_map.46.own_ref), channel_id=1, source_target_pairs={{0,2},{1,3},{2,4},{3,5},{4,6},{5,7},{6,8},{7,9},{8,10},{9,11},{10,... | collective-permute-start | bytes 786440 | tf_op jit(solution)/shard_map/ppermute | solution.py:352
  4.1 2.0 %shard_map.47 = (bf16[272,512]{1,0:T(8,128)(2,1)S(1)}, f32[128,512]{1,0:T(8,128)S(1)}, s32[8,128]{1,0:T(8,128)S(1)}, f32[128,128]{1,0:T(8,128)S(1)}, bf16[128,40...) custom-call(bf16[256,512]{1,0:T(8,128)(2,1)S(1)} %shard_map.46.own_ref, ...), custom_call_target="tpu_custom_call" | custom-call | flops 4000000000 | bytes 16000000 | tf_op jit(solution)/shard_map/pallas_call | solution.py:201
  6.2 3.1 %collective-permute-start = (bf16[272,512]{1,0:T(8,128)(2,1)S(1)}, bf16[272,512]{1,0:T(8,128)(2,1)S(1)}, u32[]{:S(2)}, u32[]{:S(2)}) collective-permute-start(bf16[272,512]{1,0:T(8,128)(2,1)S(1)} %get-tuple-element.27), channel_id=1, source_target_pairs={{0,4},{1,5},{2,6},{3,7},{4,8},{5,9},{6,10},{7,11},{8,12},{9,13},{1... | collective-permute-start | bytes 835592 | tf_op jit(solution)/shard_map/ppermute | solution.py:352
  9.3 0.9 %shard_map.48 = (s32[1,512]{1,0:T(1,128)S(1)}, f32[128,4096]{1,0:T(8,128)S(1)}, f32[128,4096]{1,0:T(8,128)S(1)}) custom-call(bf16[256,512]{1,0:T(8,128)(2,1)S(1)} %shard_map.46.own_ref, f32[128,128]{1,0:T(8,128)S(1)} %get-tuple-element.22.own_bias_ref, ...), custom_call_target="tpu_custom_call", output_to_operand_aliasing={{0}: (3, {}), {1}: (4, {}), {2}: (5, {})} | custom-call | flops 4000000000 | bytes 16000000 | tf_op jit(solution)/shard_map/pallas_call | solution.py:230
  10.3 1.6 %collective-permute-done.1.further_ref = bf16[256,512]{1,0:T(8,128)(2,1)S(1)} collective-permute-done((bf16[256,512]{1,0:T(8,128)(2,1)S(1)}, bf16[256,512]{1,0:T(8,128)(2,1)S(1)}, u32[]{:S(2)}, u32[]{:S(2)}) %collective-permute-start.1) | collective-permute-done | bytes 262176 | tf_op jit(solution)/shard_map/ppermute | solution.py:352
  11.9 3.0 %collective-permute-start.2 = (bf16[256,512]{1,0:T(8,128)(2,1)S(1)}, bf16[256,512]{1,0:T(8,128)(2,1)S(1)}, u32[]{:S(2)}, u32[]{:S(2)}) collective-permute-start(bf16[256,512]{1,0:T(8,128)(2,1)S(1)} %broadcast_select_fusion), channel_id=1, source_target_pairs={{0,1},{1,0},{2,3},{3,2},{4,5},{5,4},{6,7},{7,6},{8,9},{9,8},{10,11... | collective-permute-start | bytes 786440 | tf_op jit(solution)/shard_map/ppermute | solution.py:364
  14.8 1.2 %collective-permute-done.2.near_ref = bf16[256,512]{1,0:T(8,128)(2,1)S(1)} collective-permute-done((bf16[256,512]{1,0:T(8,128)(2,1)S(1)}, bf16[256,512]{1,0:T(8,128)(2,1)S(1)}, u32[]{:S(2)}, u32[]{:S(2)}) %collective-permute-start.2) | collective-permute-done | bytes 262176 | tf_op jit(solution)/shard_map/ppermute | solution.py:364
  16.0 3.1 %shard_map.49 = (bf16[256,512]{1,0:T(8,128)(2,1)S(1)}, f32[128,4096]{1,0:T(8,128)S(1)}, f32[128,4096]{1,0:T(8,128)S(1)}) custom-call(s32[8,128]{1,0:T(8,128)S(1)} %get-tuple-element.19.needed_ref, f32[128,512]{1,0:T(8,128)S(1)} %get-tuple-element.20.bias_ref, ...), custom_call_target="tpu_custom_call", output_to_operand_aliasing={{0}: (4, {}), {1}: (5, {}), {2}: (6, {})} | custom-call | flops 4194304 | bytes 524288 | tf_op jit(solution)/shard_map/pallas_call | solution.py:332
  19.1 0.0 collective-permute-done.further_ref
  19.1 0.4 %collective-permute-start.3 = (bf16[256,512]{1,0:T(8,128)(2,1)S(1)}, bf16[256,512]{1,0:T(8,128)(2,1)S(1)}, u32[]{:S(2)}, u32[]{:S(2)}) collective-permute-start(bf16[256,512]{1,0:T(8,128)(2,1)S(1)} %slice_select_fusion), channel_id=1, source_target_pairs={{0,1},{1,0},{2,3},{3,2},{4,5},{5,4},{6,7},{7,6},{8,9},{9,8},{10,11... | collective-permute-start | bytes 786440 | tf_op jit(solution)/shard_map/ppermute | solution.py:364
  19.6 1.2 %collective-permute-done.3.near_ref = bf16[256,512]{1,0:T(8,128)(2,1)S(1)} collective-permute-done((bf16[256,512]{1,0:T(8,128)(2,1)S(1)}, bf16[256,512]{1,0:T(8,128)(2,1)S(1)}, u32[]{:S(2)}, u32[]{:S(2)}) %collective-permute-start.3) | collective-permute-done | bytes 262176 | tf_op jit(solution)/shard_map/ppermute | solution.py:364
  20.7 2.9 %shard_map.50 = bf16[128,4096]{1,0:T(8,128)(2,1)} custom-call(s32[8,128]{1,0:T(8,128)S(1)} %get-tuple-element.19.needed_ref, f32[128,512]{1,0:T(8,128)S(1)} %get-tuple-element.20.bias_ref, bf16[128,4096]{1,0:T(8,128)(2,1)S(1)} %get-tuple-element.21.q_ref, bf16[256,512]{1,0:T(8,128)(2,1)S(1)} %collective-permute-done.3.near_ref, ...), custom_call_target="tpu_custom_call" | custom-call | flops 4194304 | bytes 524288 | tf_op jit(solution)/shard_map/pallas_call | solution.py:332
  (3 shorter events, 0.1 us)
Async XLA Ops:
  1.0 10.9 %collective-permute-start.1 = (bf16[256,512]{1,0:T(8,128)(2,1)S(1)}, bf16[256,512]{1,0:T(8,128)(2,1)S(1)}, u32[]{:S(2)}, u32[]{:S(2)}) collective-permute-start(bf16[256,512]{1,0:T(8,128)(2,1)S(1)} %shard_map.46.own_ref), channel_id=1, source_target_pairs={{0,2},{1,3},{2,4},{3,5},{4,6},{5,7},{6,8},{7,9},{8,10},{9,11},{10,... | collective-permute-start | bytes 786440 | tf_op jit(solution)/shard_map/ppermute | solution.py:352
  6.2 12.9 %collective-permute-start = (bf16[272,512]{1,0:T(8,128)(2,1)S(1)}, bf16[272,512]{1,0:T(8,128)(2,1)S(1)}, u32[]{:S(2)}, u32[]{:S(2)}) collective-permute-start(bf16[272,512]{1,0:T(8,128)(2,1)S(1)} %get-tuple-element.27), channel_id=1, source_target_pairs={{0,4},{1,5},{2,6},{3,7},{4,8},{5,9},{6,10},{7,11},{8,12},{9,13},{1... | collective-permute-start | bytes 835592 | tf_op jit(solution)/shard_map/ppermute | solution.py:352
  11.9 4.1 %collective-permute-start.2 = (bf16[256,512]{1,0:T(8,128)(2,1)S(1)}, bf16[256,512]{1,0:T(8,128)(2,1)S(1)}, u32[]{:S(2)}, u32[]{:S(2)}) collective-permute-start(bf16[256,512]{1,0:T(8,128)(2,1)S(1)} %broadcast_select_fusion), channel_id=1, source_target_pairs={{0,1},{1,0},{2,3},{3,2},{4,5},{5,4},{6,7},{7,6},{8,9},{9,8},{10,11... | collective-permute-start | bytes 786440 | tf_op jit(solution)/shard_map/ppermute | solution.py:364
  19.1 1.6 %collective-permute-start.3 = (bf16[256,512]{1,0:T(8,128)(2,1)S(1)}, bf16[256,512]{1,0:T(8,128)(2,1)S(1)}, u32[]{:S(2)}, u32[]{:S(2)}) collective-permute-start(bf16[256,512]{1,0:T(8,128)(2,1)S(1)} %slice_select_fusion), channel_id=1, source_target_pairs={{0,1},{1,0},{2,3},{3,2},{4,5},{5,4},{6,7},{7,6},{8,9},{9,8},{10,11... | collective-permute-start | bytes 786440 | tf_op jit(solution)/shard_map/ppermute | solution.py:364

commit v2 on v0

--- a/solution.py
+++ b/solution.py
@@ -13,7 +13,7 @@
 KEY_VALUE_HEADS = 4
 GROUP = QUERY_HEADS // KEY_VALUE_HEADS
 HEADS_AT_ONCE = 4
-EARLY_CHAINS = 4
+EARLY_CHAINS = 5
 EXCLUDED = -1e30
 PAD = 16
 AXES = ("dp", "ctx")

time: 23.3 us -> 23.5 us (level)
  Pallas kernels: 9.59 us -> 9.89 us
    pallas_call x1, Pallas kernels: 2.05 us -> 2.36 us  [own_part(): pl.pallas_call(functools.partial(own_kernel, rounds, rows), out_shape=(pl...]
  transfers between devices with their start and end apart: 4 -> 4, of which waited for: 4 -> 4; matrix products, arithmetic and copies ran while one was open for 0% -> 0% of each run, Pallas kernels for 25% -> 26%
where the time goes in v2:
time: 23.5 us; the launch traced here: 23.4 us
  Pallas kernels  9.89 us (42%)
  starting transfers between devices  6.97 us (30%)
  waiting for transfers between devices  6.26 us (27%)
    ppermute x2, starting transfers between devices, from_behind(): return lax.ppermute(block, AXES, [(i, i + by) for i in range(count - by)])  6.83 us
    pallas_call x2, Pallas kernels, behind_part(): pl.pallas_call(functools.partial(behind_kernel, before, last, rows), out_...  5.86 us
    ppermute x2, waiting for transfers between devices, from_behind(): return lax.ppermute(block, AXES, [(i, i + by) for i in range(count - by)])  3.21 us
    ppermute x2, waiting for transfers between devices, per_device(): lax.ppermute(jnp.where(odd == 1, further[:size], nearer[:size]), AXES, swap)  3.04 us
    pallas_call x1, Pallas kernels, own_part(): pl.pallas_call(functools.partial(own_kernel, rounds, rows), out_shape=(pl...  2.36 us
    pallas_call x1, Pallas kernels, pack(): pl.pallas_call(pack_kernel, out_shape=pltpu.VMEM((2 * rows, width), keys....  0.98 us
    pallas_call x1, Pallas kernels, own_rest(): pl.pallas_call(functools.partial(own_rest_kernel, rows), out_shape=tuple(...  0.68 us
  transfers between devices with their start and end apart: 4, of which 4 were waited for; matrix products, arithmetic and copies ran while one was open for 0% of the time, Pallas kernels for 26%

profile of v2, /device:TPU:8, one launch (start us, length us, event | category | flops | bytes accessed | tf_op | source)
XLA Modules:
  0.0 23.4 jit_solution(10208309684451123581)
XLA Ops:
  0.0 1.0 %shard_map.46.own_ref = bf16[256,512]{1,0:T(8,128)(2,1)S(1)} custom-call(bf16[128,512]{1,0:T(8,128)(2,1)} %key_hbm.1, bf16[128,512]{1,0:T(8,128)(2,1)} %value_hbm.1), custom_call_target="tpu_custom_call" | custom-call | tf_op jit(solution)/shard_map/pallas_call | solution.py:89
  1.0 3.4 %collective-permute-start.1 = (bf16[256,512]{1,0:T(8,128)(2,1)S(1)}, bf16[256,512]{1,0:T(8,128)(2,1)S(1)}, u32[]{:S(2)}, u32[]{:S(2)}) collective-permute-start(bf16[256,512]{1,0:T(8,128)(2,1)S(1)} %shard_map.46.own_ref), channel_id=1, source_target_pairs={{0,2},{1,3},{2,4},{3,5},{4,6},{5,7},{6,8},{7,9},{8,10},{9,11},{10,... | collective-permute-start | bytes 786440 | tf_op jit(solution)/shard_map/ppermute | solution.py:355
  4.4 2.4 %shard_map.47 = (bf16[272,512]{1,0:T(8,128)(2,1)S(1)}, f32[128,512]{1,0:T(8,128)S(1)}, s32[8,128]{1,0:T(8,128)S(1)}, f32[128,128]{1,0:T(8,128)S(1)}, bf16[128,40...) custom-call(bf16[256,512]{1,0:T(8,128)(2,1)S(1)} %shard_map.46.own_ref, ...), custom_call_target="tpu_custom_call" | custom-call | flops 4000000000 | bytes 16000000 | tf_op jit(solution)/shard_map/pallas_call | solution.py:204
  6.8 3.4 %collective-permute-start = (bf16[272,512]{1,0:T(8,128)(2,1)S(1)}, bf16[272,512]{1,0:T(8,128)(2,1)S(1)}, u32[]{:S(2)}, u32[]{:S(2)}) collective-permute-start(bf16[272,512]{1,0:T(8,128)(2,1)S(1)} %get-tuple-element.27), channel_id=1, source_target_pairs={{0,4},{1,5},{2,6},{3,7},{4,8},{5,9},{6,10},{7,11},{8,12},{9,13},{1... | collective-permute-start | bytes 835592 | tf_op jit(solution)/shard_map/ppermute | solution.py:355
  10.2 0.7 %shard_map.48 = (s32[1,512]{1,0:T(1,128)S(1)}, f32[128,4096]{1,0:T(8,128)S(1)}, f32[128,4096]{1,0:T(8,128)S(1)}) custom-call(bf16[256,512]{1,0:T(8,128)(2,1)S(1)} %shard_map.46.own_ref, f32[128,128]{1,0:T(8,128)S(1)} %get-tuple-element.22.own_bias_ref, ...), custom_call_target="tpu_custom_call", output_to_operand_aliasing={{0}: (3, {}), {1}: (4, {}), {2}: (5, {})} | custom-call | flops 4000000000 | bytes 16000000 | tf_op jit(solution)/shard_map/pallas_call | solution.py:233
  10.9 2.8 %collective-permute-done.1.further_ref = bf16[256,512]{1,0:T(8,128)(2,1)S(1)} collective-permute-done((bf16[256,512]{1,0:T(8,128)(2,1)S(1)}, bf16[256,512]{1,0:T(8,128)(2,1)S(1)}, u32[]{:S(2)}, u32[]{:S(2)}) %collective-permute-start.1) | collective-permute-done | bytes 262176 | tf_op jit(solution)/shard_map/ppermute | solution.py:355
  13.8 0.1 collective-permute-start.2
  13.9 1.5 %collective-permute-done.2.near_ref = bf16[256,512]{1,0:T(8,128)(2,1)S(1)} collective-permute-done((bf16[256,512]{1,0:T(8,128)(2,1)S(1)}, bf16[256,512]{1,0:T(8,128)(2,1)S(1)}, u32[]{:S(2)}, u32[]{:S(2)}) %collective-permute-start.2) | collective-permute-done | bytes 262176 | tf_op jit(solution)/shard_map/ppermute | solution.py:367
  15.4 2.9 %shard_map.49 = (bf16[256,512]{1,0:T(8,128)(2,1)S(1)}, f32[128,4096]{1,0:T(8,128)S(1)}, f32[128,4096]{1,0:T(8,128)S(1)}) custom-call(s32[8,128]{1,0:T(8,128)S(1)} %get-tuple-element.19.needed_ref, f32[128,512]{1,0:T(8,128)S(1)} %get-tuple-element.20.bias_ref, ...), custom_call_target="tpu_custom_call", output_to_operand_aliasing={{0}: (4, {}), {1}: (5, {}), {2}: (6, {})} | custom-call | flops 4194304 | bytes 524288 | tf_op jit(solution)/shard_map/pallas_call | solution.py:335
  18.3 0.4 %collective-permute-done.further_ref = bf16[272,512]{1,0:T(8,128)(2,1)S(1)} collective-permute-done((bf16[272,512]{1,0:T(8,128)(2,1)S(1)}, bf16[272,512]{1,0:T(8,128)(2,1)S(1)}, u32[]{:S(2)}, u32[]{:S(2)}) %collective-permute-start) | collective-permute-done | bytes 278560 | tf_op jit(solution)/shard_map/ppermute | solution.py:355
  18.7 0.1 collective-permute-start.3
  18.8 1.5 %collective-permute-done.3.near_ref = bf16[256,512]{1,0:T(8,128)(2,1)S(1)} collective-permute-done((bf16[256,512]{1,0:T(8,128)(2,1)S(1)}, bf16[256,512]{1,0:T(8,128)(2,1)S(1)}, u32[]{:S(2)}, u32[]{:S(2)}) %collective-permute-start.3) | collective-permute-done | bytes 262176 | tf_op jit(solution)/shard_map/ppermute | solution.py:367
  20.3 2.9 %shard_map.50 = bf16[128,4096]{1,0:T(8,128)(2,1)} custom-call(s32[8,128]{1,0:T(8,128)S(1)} %get-tuple-element.19.needed_ref, f32[128,512]{1,0:T(8,128)S(1)} %get-tuple-element.20.bias_ref, bf16[128,4096]{1,0:T(8,128)(2,1)S(1)} %get-tuple-element.21.q_ref, bf16[256,512]{1,0:T(8,128)(2,1)S(1)} %collective-permute-done.3.near_ref, ...), custom_call_target="tpu_custom_call" | custom-call | flops 4194304 | bytes 524288 | tf_op jit(solution)/shard_map/pallas_call | solution.py:335
  (3 shorter events, 0.1 us)
Async XLA Ops:
  1.0 12.8 %collective-permute-start.1 = (bf16[256,512]{1,0:T(8,128)(2,1)S(1)}, bf16[256,512]{1,0:T(8,128)(2,1)S(1)}, u32[]{:S(2)}, u32[]{:S(2)}) collective-permute-start(bf16[256,512]{1,0:T(8,128)(2,1)S(1)} %shard_map.46.own_ref), channel_id=1, source_target_pairs={{0,2},{1,3},{2,4},{3,5},{4,6},{5,7},{6,8},{7,9},{8,10},{9,11},{10,... | collective-permute-start | bytes 786440 | tf_op jit(solution)/shard_map/ppermute | solution.py:355
  6.8 11.9 %collective-permute-start = (bf16[272,512]{1,0:T(8,128)(2,1)S(1)}, bf16[272,512]{1,0:T(8,128)(2,1)S(1)}, u32[]{:S(2)}, u32[]{:S(2)}) collective-permute-start(bf16[272,512]{1,0:T(8,128)(2,1)S(1)} %get-tuple-element.27), channel_id=1, source_target_pairs={{0,4},{1,5},{2,6},{3,7},{4,8},{5,9},{6,10},{7,11},{8,12},{9,13},{1... | collective-permute-start | bytes 835592 | tf_op jit(solution)/shard_map/ppermute | solution.py:355
  13.8 1.6 %collective-permute-start.2 = (bf16[256,512]{1,0:T(8,128)(2,1)S(1)}, bf16[256,512]{1,0:T(8,128)(2,1)S(1)}, u32[]{:S(2)}, u32[]{:S(2)}) collective-permute-start(bf16[256,512]{1,0:T(8,128)(2,1)S(1)} %broadcast_select_fusion), channel_id=1, source_target_pairs={{0,1},{1,0},{2,3},{3,2},{4,5},{5,4},{6,7},{7,6},{8,9},{9,8},{10,11... | collective-permute-start | bytes 786440 | tf_op jit(solution)/shard_map/ppermute | solution.py:367
  18.7 1.6 %collective-permute-start.3 = (bf16[256,512]{1,0:T(8,128)(2,1)S(1)}, bf16[256,512]{1,0:T(8,128)(2,1)S(1)}, u32[]{:S(2)}, u32[]{:S(2)}) collective-permute-start(bf16[256,512]{1,0:T(8,128)(2,1)S(1)} %slice_select_fusion), channel_id=1, source_target_pairs={{0,1},{1,0},{2,3},{3,2},{4,5},{5,4},{6,7},{7,6},{8,9},{9,8},{10,11... | collective-permute-start | bytes 786440 | tf_op jit(solution)/shard_map/ppermute | solution.py:367

commit v3 on v0

--- a/solution.py
+++ b/solution.py
@@ -297,10 +297,16 @@
         runs = chains() if upto == rows else chains(GROUP)
         in_turn(runs, match, weigh, gather)
 
-    short = crossing <= rows // 2
-    pl.when((beyond > 0) & short)(functools.partial(attend, 2, rows // 2))
-    pl.when((beyond > 1) & jnp.logical_not(short))(functools.partial(attend, 2, rows))
-    pl.when((beyond == 1) & jnp.logical_not(short))(functools.partial(attend, 1, rows))
+    some = beyond > 0
+    quarter, half = crossing <= rows // 4, crossing <= rows // 2
+    pl.when(some & quarter)(functools.partial(attend, 2, rows // 4))
+    pl.when(some & half & jnp.logical_not(quarter))(functools.partial(attend, 2, rows // 2))
+    full = jnp.logical_not(half)
+    if last:
+        pl.when((beyond > 1) & full)(functools.partial(attend, 2, rows))
+        pl.when((beyond == 1) & full)(functools.partial(attend, 1, rows))
+    else:
+        pl.when(some & full)(functools.partial(attend, 2, rows))
 
     if last:
         @pl.when(beyond < 1)

time: 23.3 us -> 23.6 us (1.013)
  the two profiles are of different devices: /device:TPU:8 before, /device:TPU:25 now
where the time goes in v3:
time: 23.6 us; the launch traced here: 23.4 us
  starting transfers between devices  9.7 us (41%)
  Pallas kernels  9.59 us (41%)
  waiting for transfers between devices  3.95 us (17%)
    ppermute x2, starting transfers between devices, from_behind(): return lax.ppermute(block, AXES, [(i, i + by) for i in range(count - by)])  6.27 us
    pallas_call x2, Pallas kernels, behind_part(): pl.pallas_call(functools.partial(behind_kernel, before, last, rows), out_...  5.68 us
    ppermute x2, starting transfers between devices, per_device(): lax.ppermute(jnp.where(odd == 1, further[:size], nearer[:size]), AXES, swap)  3.44 us
    ppermute x2, waiting for transfers between devices, per_device(): lax.ppermute(jnp.where(odd == 1, further[:size], nearer[:size]), AXES, swap)  2.32 us
    pallas_call x1, Pallas kernels, own_part(): pl.pallas_call(functools.partial(own_kernel, rounds, rows), out_shape=(pl...  2.05 us
    ppermute x2, waiting for transfers between devices, from_behind(): return lax.ppermute(block, AXES, [(i, i + by) for i in range(count - by)])  1.62 us
    pallas_call x1, Pallas kernels, pack(): pl.pallas_call(pack_kernel, out_shape=pltpu.VMEM((2 * rows, width), keys....  0.98 us
    pallas_call x1, Pallas kernels, own_rest(): pl.pallas_call(functools.partial(own_rest_kernel, rows), out_shape=tuple(...  0.88 us
  transfers between devices with their start and end apart: 4, of which 3 were waited for; matrix products, arithmetic and copies ran while one was open for 0% of the time, Pallas kernels for 25%

profile of v3, /device:TPU:25, one launch (start us, length us, event | category | flops | bytes accessed | tf_op | source)
XLA Modules:
  0.0 23.4 jit_solution(18142738155144367578)
XLA Ops:
  0.0 1.0 %shard_map.46.own_ref = bf16[256,512]{1,0:T(8,128)(2,1)S(1)} custom-call(bf16[128,512]{1,0:T(8,128)(2,1)} %key_hbm.1, bf16[128,512]{1,0:T(8,128)(2,1)} %value_hbm.1), custom_call_target="tpu_custom_call" | custom-call | tf_op jit(solution)/shard_map/pallas_call | solution.py:89
  1.0 3.1 %collective-permute-start.1 = (bf16[256,512]{1,0:T(8,128)(2,1)S(1)}, bf16[256,512]{1,0:T(8,128)(2,1)S(1)}, u32[]{:S(2)}, u32[]{:S(2)}) collective-permute-start(bf16[256,512]{1,0:T(8,128)(2,1)S(1)} %shard_map.46.own_ref), channel_id=1, source_target_pairs={{0,2},{1,3},{2,4},{3,5},{4,6},{5,7},{6,8},{7,9},{8,10},{9,11},{10,... | collective-permute-start | bytes 786440 | tf_op jit(solution)/shard_map/ppermute | solution.py:361
  4.1 2.0 %shard_map.47 = (bf16[272,512]{1,0:T(8,128)(2,1)S(1)}, f32[128,512]{1,0:T(8,128)S(1)}, s32[8,128]{1,0:T(8,128)S(1)}, f32[128,128]{1,0:T(8,128)S(1)}, bf16[128,40...) custom-call(bf16[256,512]{1,0:T(8,128)(2,1)S(1)} %shard_map.46.own_ref, ...), custom_call_target="tpu_custom_call" | custom-call | flops 4000000000 | bytes 16000000 | tf_op jit(solution)/shard_map/pallas_call | solution.py:204
  6.2 3.1 %collective-permute-start = (bf16[272,512]{1,0:T(8,128)(2,1)S(1)}, bf16[272,512]{1,0:T(8,128)(2,1)S(1)}, u32[]{:S(2)}, u32[]{:S(2)}) collective-permute-start(bf16[272,512]{1,0:T(8,128)(2,1)S(1)} %get-tuple-element.27), channel_id=1, source_target_pairs={{0,4},{1,5},{2,6},{3,7},{4,8},{5,9},{6,10},{7,11},{8,12},{9,13},{1... | collective-permute-start | bytes 835592 | tf_op jit(solution)/shard_map/ppermute | solution.py:361
  9.3 0.9 %shard_map.48 = (s32[1,512]{1,0:T(1,128)S(1)}, f32[128,4096]{1,0:T(8,128)S(1)}, f32[128,4096]{1,0:T(8,128)S(1)}) custom-call(bf16[256,512]{1,0:T(8,128)(2,1)S(1)} %shard_map.46.own_ref, f32[128,128]{1,0:T(8,128)S(1)} %get-tuple-element.22.own_bias_ref, ...), custom_call_target="tpu_custom_call", output_to_operand_aliasing={{0}: (3, {}), {1}: (4, {}), {2}: (5, {})} | custom-call | flops 4000000000 | bytes 16000000 | tf_op jit(solution)/shard_map/pallas_call | solution.py:233
  10.2 1.6 %collective-permute-done.1.further_ref = bf16[256,512]{1,0:T(8,128)(2,1)S(1)} collective-permute-done((bf16[256,512]{1,0:T(8,128)(2,1)S(1)}, bf16[256,512]{1,0:T(8,128)(2,1)S(1)}, u32[]{:S(2)}, u32[]{:S(2)}) %collective-permute-start.1) | collective-permute-done | bytes 262176 | tf_op jit(solution)/shard_map/ppermute | solution.py:361
  11.9 3.0 %collective-permute-start.2 = (bf16[256,512]{1,0:T(8,128)(2,1)S(1)}, bf16[256,512]{1,0:T(8,128)(2,1)S(1)}, u32[]{:S(2)}, u32[]{:S(2)}) collective-permute-start(bf16[256,512]{1,0:T(8,128)(2,1)S(1)} %broadcast_select_fusion), channel_id=1, source_target_pairs={{0,1},{1,0},{2,3},{3,2},{4,5},{5,4},{6,7},{7,6},{8,9},{9,8},{10,11... | collective-permute-start | bytes 786440 | tf_op jit(solution)/shard_map/ppermute | solution.py:373
  14.8 1.2 %collective-permute-done.2.near_ref = bf16[256,512]{1,0:T(8,128)(2,1)S(1)} collective-permute-done((bf16[256,512]{1,0:T(8,128)(2,1)S(1)}, bf16[256,512]{1,0:T(8,128)(2,1)S(1)}, u32[]{:S(2)}, u32[]{:S(2)}) %collective-permute-start.2) | collective-permute-done | bytes 262176 | tf_op jit(solution)/shard_map/ppermute | solution.py:373
  16.0 2.9 %shard_map.49 = (bf16[256,512]{1,0:T(8,128)(2,1)S(1)}, f32[128,4096]{1,0:T(8,128)S(1)}, f32[128,4096]{1,0:T(8,128)S(1)}) custom-call(s32[8,128]{1,0:T(8,128)S(1)} %get-tuple-element.19.needed_ref, f32[128,512]{1,0:T(8,128)S(1)} %get-tuple-element.20.bias_ref, ...), custom_call_target="tpu_custom_call", output_to_operand_aliasing={{0}: (4, {}), {1}: (5, {}), {2}: (6, {})} | custom-call | flops 4194304 | bytes 524288 | tf_op jit(solution)/shard_map/pallas_call | solution.py:341
  18.9 0.0 collective-permute-done.further_ref
  19.0 0.5 %collective-permute-start.3 = (bf16[256,512]{1,0:T(8,128)(2,1)S(1)}, bf16[256,512]{1,0:T(8,128)(2,1)S(1)}, u32[]{:S(2)}, u32[]{:S(2)}) collective-permute-start(bf16[256,512]{1,0:T(8,128)(2,1)S(1)} %slice_select_fusion), channel_id=1, source_target_pairs={{0,1},{1,0},{2,3},{3,2},{4,5},{5,4},{6,7},{7,6},{8,9},{9,8},{10,11... | collective-permute-start | bytes 786440 | tf_op jit(solution)/shard_map/ppermute | solution.py:373
  19.5 1.2 %collective-permute-done.3.near_ref = bf16[256,512]{1,0:T(8,128)(2,1)S(1)} collective-permute-done((bf16[256,512]{1,0:T(8,128)(2,1)S(1)}, bf16[256,512]{1,0:T(8,128)(2,1)S(1)}, u32[]{:S(2)}, u32[]{:S(2)}) %collective-permute-start.3) | collective-permute-done | bytes 262176 | tf_op jit(solution)/shard_map/ppermute | solution.py:373
  20.6 2.8 %shard_map.50 = bf16[128,4096]{1,0:T(8,128)(2,1)} custom-call(s32[8,128]{1,0:T(8,128)S(1)} %get-tuple-element.19.needed_ref, f32[128,512]{1,0:T(8,128)S(1)} %get-tuple-element.20.bias_ref, bf16[128,4096]{1,0:T(8,128)(2,1)S(1)} %get-tuple-element.21.q_ref, bf16[256,512]{1,0:T(8,128)(2,1)S(1)} %collective-permute-done.3.near_ref, ...), custom_call_target="tpu_custom_call" | custom-call | flops 4194304 | bytes 524288 | tf_op jit(solution)/shard_map/pallas_call | solution.py:341
  (3 shorter events, 0.1 us)
Async XLA Ops:
  1.0 10.9 %collective-permute-start.1 = (bf16[256,512]{1,0:T(8,128)(2,1)S(1)}, bf16[256,512]{1,0:T(8,128)(2,1)S(1)}, u32[]{:S(2)}, u32[]{:S(2)}) collective-permute-start(bf16[256,512]{1,0:T(8,128)(2,1)S(1)} %shard_map.46.own_ref), channel_id=1, source_target_pairs={{0,2},{1,3},{2,4},{3,5},{4,6},{5,7},{6,8},{7,9},{8,10},{9,11},{10,... | collective-permute-start | bytes 786440 | tf_op jit(solution)/shard_map/ppermute | solution.py:361
  6.2 12.8 %collective-permute-start = (bf16[272,512]{1,0:T(8,128)(2,1)S(1)}, bf16[272,512]{1,0:T(8,128)(2,1)S(1)}, u32[]{:S(2)}, u32[]{:S(2)}) collective-permute-start(bf16[272,512]{1,0:T(8,128)(2,1)S(1)} %get-tuple-element.27), channel_id=1, source_target_pairs={{0,4},{1,5},{2,6},{3,7},{4,8},{5,9},{6,10},{7,11},{8,12},{9,13},{1... | collective-permute-start | bytes 835592 | tf_op jit(solution)/shard_map/ppermute | solution.py:361
  11.9 4.1 %collective-permute-start.2 = (bf16[256,512]{1,0:T(8,128)(2,1)S(1)}, bf16[256,512]{1,0:T(8,128)(2,1)S(1)}, u32[]{:S(2)}, u32[]{:S(2)}) collective-permute-start(bf16[256,512]{1,0:T(8,128)(2,1)S(1)} %broadcast_select_fusion), channel_id=1, source_target_pairs={{0,1},{1,0},{2,3},{3,2},{4,5},{5,4},{6,7},{7,6},{8,9},{9,8},{10,11... | collective-permute-start | bytes 786440 | tf_op jit(solution)/shard_map/ppermute | solution.py:373
  19.0 1.6 %collective-permute-start.3 = (bf16[256,512]{1,0:T(8,128)(2,1)S(1)}, bf16[256,512]{1,0:T(8,128)(2,1)S(1)}, u32[]{:S(2)}, u32[]{:S(2)}) collective-permute-start(bf16[256,512]{1,0:T(8,128)(2,1)S(1)} %slice_select_fusion), channel_id=1, source_target_pairs={{0,1},{1,0},{2,3},{3,2},{4,5},{5,4},{6,7},{7,6},{8,9},{9,8},{10,11... | collective-permute-start | bytes 786440 | tf_op jit(solution)/shard_map/ppermute | solution.py:373
